TPU v7x, 128 devices: a whole 4x4x4 slice. The times are simulated.
128 devices in a mesh: mom: 8 (over y, core), pair: 16 (over x, z).
Axes of the slice: x: 4, y: 4, z: 4, core: 2. Of those that a mesh axis runs over, the one named last changes fastest.
Arguments:
- blocks: bfloat16 [8, 16, 1024, 1024], P('mom', None, 'pair'), may hold values from -1.078125 to 1.078125
- left_ids: int32 [8, 48], P('mom', 'pair'), may hold values from 0 to 15
- right_ids: int32 [8, 48], P('mom', 'pair'), may hold values from 0 to 15
- slice_ids: int32 [8, 48], P('mom', 'pair'), may hold values from 0 to 1
- weight_ids: int32 [8, 48], P('mom', 'pair'), may hold values from 0 to 7
- counts: int32 [8, 16], P('mom', 'pair'), may hold values from 1 to 3, 32 in all within a row
- subduction: float32 [8], replicated, may hold values from -1 to 1
Outputs:
- operator: float32 [8, 1024, 2, 1024], P('mom', 'pair')
Inputs may be any that keep to these rules, and one draw needn't show every extreme that they name: Each row of counts sums to exactly 32.
All inputs are finite; a program needn't handle non-finite values. No bound on the sum of `counts` on one device may be relied on, other than what follows from the above.
Results may differ from a plain program's by a relative error of at most 0.0029.
Values may be sent and summed in bfloat16 or wider, within the bound.
A program may use at most 128 MiB of HBM per device.

v0:
```python
import jax
import jax.numpy as jnp
from jax import lax
from jax.sharding import PartitionSpec as P

PAIR_DEV = 3
SLICES = 2


def partner_2(shard, axis, apart):
    return lax.ppermute(shard, axis, [(i, i ^ 1 << apart) for i in range(lax.axis_size(axis))])


def mixing_table(lefts, rights, slices, weights, allowed, subduction, families):
    total_slots = lefts.shape[0]
    slot = jnp.arange(total_slots, dtype=jnp.int32)
    list_of = slot // PAIR_DEV
    lists = jnp.arange(allowed.shape[0], dtype=jnp.int32)
    limit = jnp.sum(jnp.where(list_of[:, None] == lists[None, :], allowed[None, :], 0), axis=1)
    live = slot % PAIR_DEV < limit
    table_ids = jnp.arange(subduction.shape[0], dtype=jnp.int32)
    looked = jnp.sum(
        jnp.where(weights[:, None] == table_ids[None, :], subduction[None, :], 0.0), axis=1
    )
    select = (slices[:, None] == jnp.arange(SLICES, dtype=jnp.int32)[None, :]).astype(jnp.float32)
    scales = jnp.where(live, looked, 0.0)[:, None] * select
    fam_ids = jnp.arange(families, dtype=jnp.int32)
    right_hot = (rights[:, None] == fam_ids[None, :]).astype(jnp.float32)
    left_hot = (lefts[:, None] == fam_ids[None, :]).astype(jnp.float32)
    return jnp.einsum("kt,kb,ka->tba", scales, right_hot, left_hot, precision=lax.Precision.HIGHEST)


def combine_left(mixing, panels):
    families = panels.shape[0]
    flat = panels.astype(jnp.float32).reshape(families, -1)
    mixed = jnp.dot(
        mixing.reshape(SLICES * families, families), flat, precision=lax.Precision.HIGHEST
    )
    return mixed.astype(jnp.bfloat16).reshape((SLICES, families) + panels.shape[1:])


def body(blocks, left_ids, right_ids, slice_ids, weight_ids, counts, subduction):
    gathered = (
        lax.all_gather(left_ids, "pair", axis=1, tiled=True),
        lax.all_gather(right_ids, "pair", axis=1, tiled=True),
        lax.all_gather(slice_ids, "pair", axis=1, tiled=True),
        lax.all_gather(weight_ids, "pair", axis=1, tiled=True),
        lax.all_gather(counts, "pair", axis=1, tiled=True),
    )
    own = blocks[0]
    families = own.shape[0]
    mixing = mixing_table(
        gathered[0][0],
        gathered[1][0],
        gathered[2][0],
        gathered[3][0],
        gathered[4][0],
        subduction,
        families,
    )
    partner = partner_2(own, "mom", 0)
    combined = combine_left(mixing, own)
    result = jnp.einsum(
        "tbij,bjl->itl",
        combined,
        lax.all_gather(partner, "pair", axis=1, tiled=True),
        preferred_element_type=jnp.float32,
    )
    return result.reshape((1,) + result.shape)


def solution(mesh):
    return jax.shard_map(
        body,
        mesh=mesh,
        in_specs=(
            P("mom", None, "pair", None),
            P("mom", "pair"),
            P("mom", "pair"),
            P("mom", "pair"),
            P("mom", "pair"),
            P("mom", "pair"),
            P(),
        ),
        out_specs=P("mom", "pair", None, None),
        check_vma=False,
    )
```

profile of v0, /device:TPU:1, one launch (start us, length us, event | category | flops | bytes accessed | tf_op | source)
XLA Modules:
  0.0 235.2 jit_solution(4597328169797305027)
XLA Ops:
  6.5 0.0 copy-start.1
  6.5 0.0 copy-start.2
  6.5 0.0 copy-start.3
  6.5 0.0 copy-start.4
  6.5 0.0 copy-start.5
  6.6 0.0 all-gather.2.cloned.1.call-start
  6.6 1.5 collective-permute-start
  8.1 4.0 %collective-permute-done = bf16[16,64,1024]{2,1,0:T(8,128)(2,1)S(1)} collective-permute-done((bf16[16,64,1024]{2,1,0:T(8,128)(2,1)}, bf16[16,64,1024]{2,1,0:T(8,128)(2,1)S(1)}, u32[]{:S(2)}, u32[]{:S(2)}) %collective-permute-start) | collective-permute-done | bytes 2097184 | tf_op jit(solution)/shard_map/ppermute | solution.py:11
  12.1 1.3 copy-done
  13.4 0.0 all-gather.2.cloned.1.call-update
  14.1 2.7 %copy.11 = bf16[2,8,64,1024]{3,1,2,0:T(8,128)(2,1)S(1)} copy(bf16[2,8,64,1024]{3,2,1,0:T(8,128)(2,1)} %bitcast.49) | data formatting | bytes 4194304
  16.8 0.0 copy-done.6
  16.9 0.6 dynamic-slice
  18.1 0.7 bitcast_dynamic-update-slice_fusion.2
  18.8 0.0 copy-done.1
  18.8 0.1 bitcast_dynamic-update-slice_fusion.4
  18.9 0.0 copy-done.2
  18.9 0.1 bitcast_dynamic-update-slice_fusion.1
  19.0 0.0 copy-done.3
  19.0 0.1 bitcast_dynamic-update-slice_fusion.3
  19.1 0.0 copy-done.4
  19.1 0.1 bitcast_dynamic-update-slice_fusion
  19.2 13.6 %all-reduce.5 = (s32[48]{0:T(128)S(1)}, s32[48]{0:T(128)S(1)}, s32[16]{0:T(128)S(1)}, s32[48]{0:T(128)S(1)}, s32[48]{0:T(128)S(1)}) all-reduce(s32[48]{0:T(128)S(1)} %bitcast_dynamic-update-slice_fusion.3, s32[48]{0:T(128)S(1)} %bitcast_dynamic-update-slice_fusion.1, ...), channel_id=1, replica_groups=mesh['mom'=8,'pair'=16] {'pair'}, use_global_device_ids=true, to_apply=%add.1 | all-reduce | flops 208 | bytes 1664
  32.9 0.0 copy-done.5
  32.9 0.1 select_reduce_fusion.1
  32.9 0.1 select_reduce_fusion
  33.1 0.1 fusion.8
  33.2 3.6 %convolution_convert_fusion = bf16[32,65536]{1,0:T(8,128)(2,1)S(1)} fusion(f32[32,16]{1,0:T(8,128)S(1)} %bitcast.50, bf16[16,65536]{1,0:T(8,128)(2,1)S(1)} %bitcast.47), kind=kOutput, calls=%fused_computation | convolution fusion | flops 404750336 | bytes 6293504 | tf_op jit(solution)/shard_map/dot_general | solution.py:36
  36.8 4.4 %copy.12 = bf16[4,8,64,1024]{3,2,1,0:T(8,128)(2,1)} copy(bf16[4,8,64,1024]{3,1,2,0:T(8,128)(2,1)S(1)} %bitcast.46) | data formatting | bytes 8388608
  41.1 171.9 %all-gather.2.cloned.1.call-done = bf16[16,1024,1024]{2,1,0:T(8,128)(2,1)} async-done(((bf16[16,64,1024]{2,1,0:T(8,128)(2,1)}), bf16[16,1024,1024]{2,1,0:T(8,128)(2,1)}) %all-gather.2.cloned.1.call-update) | async-done | bytes 33554448 | tf_op jit(solution)/shard_map/all_gather | solution.py:66
  213.0 14.1 %fusion.3 = f32[1,64,2,1024]{3,1,2,0:T(8,128)S(1)} fusion(bf16[16,1024,1024]{2,1,0:T(8,128)(2,1)} %all-gather.2.cloned.1.call-done, bf16[2,16,64,1024]{3,2,1,0:T(8,128)(2,1)} %bitcast.45), kind=kOutput, calls=%fused_computation.4 | convolution fusion | flops 4294967296 | bytes 38273024 | tf_op jit(solution)/shard_map/tbij,bjl->itl/dot_general | solution.py:63
  227.1 1.2 copy.9
  (11 shorter events, 0.0 us)
Async XLA Ops:
  6.5 10.3 %copy-start.6 = (u32[128]{0:T(128)S(1)}, u32[128]{0:T(128)}, u32[]{:S(2)}) copy-start(u32[128]{0:T(128)} %constant.32) | copy-start | bytes 1540
  6.5 12.3 %copy-start.1 = (s32[1,3]{1,0:T(1,128)S(1)}, s32[1,3]{1,0:T(1,128)}, u32[]{:S(2)}) copy-start(s32[1,3]{1,0:T(1,128)} %param.9) | copy-start | bytes 40
  6.5 12.4 %copy-start.2 = (s32[1,3]{1,0:T(1,128)S(1)}, s32[1,3]{1,0:T(1,128)}, u32[]{:S(2)}) copy-start(s32[1,3]{1,0:T(1,128)} %param.11) | copy-start | bytes 40
  6.5 12.5 %copy-start.3 = (s32[1,3]{1,0:T(1,128)S(1)}, s32[1,3]{1,0:T(1,128)}, u32[]{:S(2)}) copy-start(s32[1,3]{1,0:T(1,128)} %param.10) | copy-start | bytes 40
  6.5 12.6 %copy-start.4 = (s32[1,3]{1,0:T(1,128)S(1)}, s32[1,3]{1,0:T(1,128)}, u32[]{:S(2)}) copy-start(s32[1,3]{1,0:T(1,128)} %param.8) | copy-start | bytes 40
  6.5 26.3 %copy-start.5 = (f32[8]{0:T(128)S(1)}, f32[8]{0:T(128)}, u32[]{:S(2)}) copy-start(f32[8]{0:T(128)} %param.13) | copy-start | bytes 100
  6.6 206.5 %all-gather.2.cloned.1.call-start = ((), (), s32[]{:S(2)}) async-start(), calls=%async_computation | async-start | bytes 35651584 | tf_op jit(solution)/shard_map/all_gather | solution.py:66
  6.6 5.5 %collective-permute-start = (bf16[16,64,1024]{2,1,0:T(8,128)(2,1)}, bf16[16,64,1024]{2,1,0:T(8,128)(2,1)S(1)}, u32[]{:S(2)}, u32[]{:S(2)}) collective-permute-start(bf16[16,64,1024]{2,1,0:T(8,128)(2,1)} %bitcast.48), channel_id=1, source_target_pairs={{0,16},{16,0},{32,48},{48,32},{64,80},{80,64},{96,112},{112,96},{1... | collective-permute-start | bytes 6291464 | tf_op jit(solution)/shard_map/ppermute | solution.py:11
  12.1 1.3 copy-start
Sparse Core Ops, SparseCore 0:
  13.6 199.4 all-gather.1
where the time goes:
time: 235 us
  waiting for transfers between devices  176 us (75%)
  matrix products  17.8 us (8%)
  between operations  14.8 us (6%)
  blocking collectives  13.6 us (6%)
  local copies, waits for them, and re-layouts  11.3 us (5%)
    all_gather x1, waiting for transfers between devices, body(): lax.all_gather(partner, 'pair', axis=1, tiled=True)  172 us
    dot_general x1, matrix products, body(): jnp.einsum('tbij,bjl->itl', combined, lax.all_gather(partner, 'pair', axi...  14.1 us
    unnamed x1, blocking collectives  13.6 us
    unnamed x27, local copies, waits for them, and re-layouts  10.1 us
  transfers between devices with their start and end apart: 2, of which 2 were waited for; matrix products, arithmetic and copies ran while one was open for 5% of the time, Pallas kernels for 0%

commit v1 on v0

--- a/solution.py
+++ b/solution.py
@@ -63,7 +63,15 @@
     result = jnp.einsum(
         "tbij,bjl->itl",
         combined,
-        lax.all_gather(partner, "pair", axis=1, tiled=True),
+        jnp.concatenate(
+            lax.all_to_all(
+                jnp.stack([partner for _ in range(lax.axis_size("pair"))]),
+                axis_name="pair",
+                split_axis=0,
+                concat_axis=0,
+            ),
+            axis=1,
+        ),
         preferred_element_type=jnp.float32,
     )
     return result.reshape((1,) + result.shape)

time: 235 us -> 699 us (2.97)
  blocking collectives: 13.6 us -> 617 us
  waiting for transfers between devices: 176 us -> 4 us
  local copies, waits for them, and re-layouts: 11.3 us -> 44 us
  between operations: 14.8 us -> 1.48 us
  starting transfers between devices: 1.54 us -> 9.15 us
    unnamed x1, blocking collectives: 13.6 us -> 617 us
    all_gather x1 -> x0, waiting for transfers between devices: 172 us -> none  [body(): lax.all_gather(partner, 'pair', axis=1, tiled=True)]
    reshape x0 -> x1, local copies, waits for them, and re-layouts: none -> 23.1 us  [body(): jnp.concatenate(lax.all_to_all(jnp.stack([partner for _ in range(lax.axis...]
    another operation x0 -> x1, local copies, waits for them, and re-layouts: none -> 11 us  [body(): jnp.stack([partner for _ in range(lax.axis_size('pair'))])]
    all_to_all x0 -> x1, starting transfers between devices: none -> 7.73 us  [body(): lax.all_to_all(jnp.stack([partner for _ in range(lax.axis_size('pair'))])...]
  transfers between devices with their start and end apart: 2 -> 2, of which waited for: 2 -> 1; matrix products, arithmetic and copies ran while one was open for 5% -> 2% of each run, Pallas kernels for 0% -> 0%
where the time goes in v1:
time: 699 us; the launch traced here: 693 us
  blocking collectives  617 us (88%)
  local copies, waits for them, and re-layouts  44 us (6%)
  matrix products  17.8 us (3%)
  starting transfers between devices  9.15 us (1%)
    unnamed x1, blocking collectives  617 us
    reshape x1, local copies, waits for them, and re-layouts, body(): jnp.concatenate(lax.all_to_all(jnp.stack([partner for _ in range(lax.axis...  23.1 us
    dot_general x1, matrix products, body(): jnp.einsum('tbij,bjl->itl', combined, jnp.concatenate(lax.all_to_all(jnp....  14.1 us
  transfers between devices with their start and end apart: 2, of which 1 were waited for; matrix products, arithmetic and copies ran while one was open for 2% of the time, Pallas kernels for 0%

profile of v1, /device:TPU:1, one launch (start us, length us, event | category | flops | bytes accessed | tf_op | source)
XLA Modules:
  0.0 693.4 jit_solution(12767800785091776527)
XLA Ops:
  0.0 1.4 collective-permute-start
  1.4 4.0 collective-permute-done
  5.4 11.0 %stack.2 = bf16[16,16,64,1024]{3,2,1,0:T(8,128)(2,1)} broadcast(bf16[16,64,1024]{2,1,0:T(8,128)(2,1)S(1)} %collective-permute-done), dimensions={1,2,3} | broadcast | bytes 35651584 | tf_op jit(solution)/shard_map/stack | solution.py:68
  16.4 7.7 %all-to-all-start = ((bf16[16,16,64,1024]{3,2,1,0:T(8,128)(2,1)}), bf16[16,16,64,1024]{3,2,1,0:T(8,128)(2,1)}, u32[]{:S(2)}, u32[]{:S(2)}) async-start(bf16[16,16,64,1024]{3,2,1,0:T(8,128)(2,1)} %stack.2), calls=%async_computation | async-start | bytes 67108864 | tf_op jit(solution)/shard_map/all_to_all | solution.py:67
  24.2 0.0 copy-start.5
  24.2 0.0 copy-start
  24.2 0.0 copy-start.1
  24.2 0.0 copy-start.2
  24.2 0.0 copy-start.3
  24.2 0.0 copy-start.4
  24.9 2.7 copy.14
  27.7 0.0 copy-done.5
  27.7 0.6 dynamic-slice
  28.9 0.7 bitcast_dynamic-update-slice_fusion.2
  29.6 0.0 copy-done
  29.6 0.1 bitcast_dynamic-update-slice_fusion.3
  29.7 0.0 copy-done.1
  29.7 0.1 bitcast_dynamic-update-slice_fusion.1
  29.8 0.0 copy-done.2
  29.8 0.1 bitcast_dynamic-update-slice_fusion.4
  29.9 0.0 copy-done.3
  29.9 0.1 bitcast_dynamic-update-slice_fusion
  30.0 616.7 %all-reduce.5 = (s32[48]{0:T(128)S(1)}, s32[48]{0:T(128)S(1)}, s32[16]{0:T(128)S(1)}, s32[48]{0:T(128)S(1)}, s32[48]{0:T(128)S(1)}) all-reduce(s32[48]{0:T(128)S(1)} %bitcast_dynamic-update-slice_fusion.3, s32[48]{0:T(128)S(1)} %bitcast_dynamic-update-slice_fusion.1, ...), channel_id=1, replica_groups=mesh['mom'=8,'pair'=16] {'pair'}, use_global_device_ids=true, to_apply=%add.1 | all-reduce | flops 208 | bytes 1664
  646.8 0.1 select_reduce_fusion.1
  646.9 0.1 select_reduce_fusion
  647.0 0.1 fusion.5
  647.1 3.6 convolution_convert_fusion
  650.7 4.3 copy.15
  655.0 0.0 all-to-all-done
  655.0 23.1 %copy.11 = bf16[16,16,64,1024]{3,2,1,0:T(8,128)(2,1)} copy(bf16[16,16,64,1024]{3,2,0,1:T(8,128)(2,1)} %bitcast.11) | data formatting | bytes 67108864 | tf_op jit(solution)/shard_map/reshape | solution.py:66
  678.1 14.1 %fusion.2 = f32[1,64,2,1024]{3,1,2,0:T(8,128)S(1)} fusion(bf16[16,1024,1024,1]{2,1,0,3:T(8,128)(2,1)} %bitcast.45, bf16[2,16,64,1024]{3,2,1,0:T(8,128)(2,1)} %bitcast.46), kind=kOutput, calls=%fused_computation.3 | convolution fusion | flops 4294967296 | bytes 38273024 | tf_op jit(solution)/shard_map/tbij,bjl->itl/dot_general | solution.py:63
  692.2 1.2 copy.12
  (10 shorter events, 0.0 us)
Async XLA Ops:
  0.0 5.4 collective-permute-start
  16.4 638.6 %all-to-all-start = ((bf16[16,16,64,1024]{3,2,1,0:T(8,128)(2,1)}), bf16[16,16,64,1024]{3,2,1,0:T(8,128)(2,1)}, u32[]{:S(2)}, u32[]{:S(2)}) async-start(bf16[16,16,64,1024]{3,2,1,0:T(8,128)(2,1)} %stack.2), calls=%async_computation | async-start | bytes 67108864 | tf_op jit(solution)/shard_map/all_to_all | solution.py:67
  24.2 3.5 copy-start.5
  24.2 5.4 copy-start
  24.2 5.5 copy-start.1
  24.2 5.6 copy-start.2
  24.2 5.7 copy-start.3
  24.2 622.5 %copy-start.4 = (f32[8]{0:T(128)S(1)}, f32[8]{0:T(128)}, u32[]{:S(2)}) copy-start(f32[8]{0:T(128)} %param.13) | copy-start | bytes 100
